TPU v7x, 512 devices: a whole 4x8x8 slice. The times are simulated.
512 devices in a mesh: dp: 64 (over z, x, core), seq: 8 (over y).
Axes of the slice: x: 4, y: 8, z: 8, core: 2. Of those that a mesh axis runs over, the one named last changes fastest.
Arguments:
- queries: bfloat16 [65536, 4096], P(('dp', 'seq')), may hold values from -6 to 6
- keys: bfloat16 [65536, 512], P(('dp', 'seq')), may hold values from -6 to 6
- values: bfloat16 [65536, 512], P(('dp', 'seq')), may hold values from -6 to 6
- grad_out: bfloat16 [65536, 4096], P(('dp', 'seq')), may hold values from -6 to 6
- quant_scale: float32 [2, 4, 128], replicated, may hold values from 2 to 8
- doc_lengths: int32 [64, 8], P('dp'), may hold values from 1 to 512, as said below
Outputs:
- attn_out: bfloat16 [65536, 4096], P(('dp', 'seq'))
- grad_queries: bfloat16 [65536, 4096], P(('dp', 'seq'))
- grad_keys: bfloat16 [65536, 512], P(('dp', 'seq'))
- grad_values: bfloat16 [65536, 512], P(('dp', 'seq'))
- grad_scale: float32 [2, 4, 128], replicated
Inputs may be any that keep to these rules, and one draw needn't show every extreme that they name: `doc_lengths`: each row sums to 1024; its largest length is exactly 512.
All inputs are finite; a program needn't handle non-finite values.
Results may differ from a plain program's by a relative error of at most 0.04.
Values may be sent and summed in bfloat16 or wider, within the bound.
A program may use at most 64 MiB of HBM per device.

v0:
```python
import math
import jax
import jax.numpy as jnp
from jax import lax
from jax.sharding import PartitionSpec as P

two_pi = 2.0 * math.pi


def quantize(source, clip):
    level = 127.0 * jnp.tanh(source / clip)
    return clip / 127.0 * (level - jnp.sin(two_pi * level) / two_pi)


def quant_pair(key_raw, value_raw, clip):
    return (quantize(key_raw, clip[0]), quantize(value_raw, clip[1]))


def segments(lengths, length):
    ends = jnp.cumsum(lengths)
    positions = jnp.arange(length, dtype=jnp.int32)
    return jnp.sum((positions[:, None] >= ends[None, :]).astype(jnp.int32), axis=1)


def attend(query_rows, key_rows, value_rows, grad_rows, segment, row_start, local_kv):
    length = query_rows.shape[0]
    key_len = key_rows.shape[0]
    head_dim = key_rows.shape[1] // local_kv
    per_group = query_rows.shape[1] // (local_kv * head_dim)
    query4 = query_rows.reshape(length, local_kv, per_group, head_dim)
    grad4 = grad_rows.reshape(length, local_kv, per_group, head_dim)
    key3 = key_rows.reshape(key_len, local_kv, head_dim)
    value3 = value_rows.reshape(key_len, local_kv, head_dim)
    block = min(512, length)
    scale = head_dim ** (-0.5)
    columns = jnp.arange(key_len, dtype=jnp.int32)

    def step(carry, index):
        key_acc, value_acc = carry
        start = index * block
        query_blk = lax.dynamic_slice_in_dim(query4, start, block, 0)
        grad_blk = lax.dynamic_slice_in_dim(grad4, start, block, 0)
        row_ids = row_start + start + jnp.arange(block, dtype=jnp.int32)
        row_seg = lax.dynamic_slice_in_dim(segment, row_start + start, block, 0)
        allowed = (columns[None, :] <= row_ids[:, None]) & (segment[None, :] == row_seg[:, None])
        scores = (
            jnp.einsum("qngd,knd->ngqk", query_blk, key3, preferred_element_type=jnp.float32)
            * scale
        )
        scores = jnp.where(allowed, scores, -1e30)
        weights = jnp.exp(scores - jnp.max(scores, axis=-1, keepdims=True))
        probs = weights / jnp.sum(weights, axis=-1, keepdims=True)
        probs_b = probs.astype(jnp.bfloat16)
        output = jnp.einsum(
            "ngqk,knd->qngd", probs_b, value3, preferred_element_type=jnp.float32
        ).astype(jnp.bfloat16)
        delta = jnp.transpose(
            jnp.sum(grad_blk.astype(jnp.float32) * output.astype(jnp.float32), axis=-1), (1, 2, 0)
        )
        dprob = jnp.einsum("qngd,knd->ngqk", grad_blk, value3, preferred_element_type=jnp.float32)
        dscore = (probs * (dprob - delta[..., None]) * scale).astype(jnp.bfloat16)
        grad_query = jnp.einsum(
            "ngqk,knd->qngd", dscore, key3, preferred_element_type=jnp.float32
        ).astype(jnp.bfloat16)
        key_acc = key_acc + jnp.einsum(
            "ngqk,qngd->knd", dscore, query_blk, preferred_element_type=jnp.float32
        )
        value_acc = value_acc + jnp.einsum(
            "ngqk,qngd->knd", probs_b, grad_blk, preferred_element_type=jnp.float32
        )
        return ((key_acc, value_acc), (output, grad_query))

    zeros = jnp.zeros((key_len, local_kv, head_dim), jnp.float32)
    (key_grad, value_grad), (outputs, grad_query) = lax.scan(
        step, (zeros, zeros), jnp.arange(length // block, dtype=jnp.int32)
    )
    return (
        outputs.reshape(length, -1),
        grad_query.reshape(length, -1),
        key_grad.reshape(key_len, -1),
        value_grad.reshape(key_len, -1),
    )


def on_device(queries, keys, values, grad_out, quant_scale, doc_lengths):
    tok_rows = queries.shape[0]
    seq_count = lax.axis_size("seq")
    kv_heads = quant_scale.shape[1]
    head_dim = quant_scale.shape[2]
    slab_rows = tok_rows * seq_count
    segment = segments(doc_lengths[0], slab_rows)
    key_raw = keys.astype(jnp.float32).reshape(tok_rows, kv_heads, head_dim)
    value_raw = values.astype(jnp.float32).reshape(tok_rows, kv_heads, head_dim)
    (key_q, value_q), pull_tokens = jax.vjp(quant_pair, key_raw, value_raw, quant_scale)
    send_key = key_q.astype(jnp.bfloat16).reshape(tok_rows, kv_heads * head_dim)
    send_value = value_q.astype(jnp.bfloat16).reshape(tok_rows, kv_heads * head_dim)
    repeats = max(1, seq_count // kv_heads)
    local_kv = max(1, kv_heads // seq_count)
    query_h, grad_h = (
        lax.all_to_all(queries, "seq", split_axis=1, concat_axis=0, tiled=True),
        lax.all_to_all(grad_out, "seq", split_axis=1, concat_axis=0, tiled=True),
    )

    def widen(array):
        spread = jnp.broadcast_to(
            array.reshape(tok_rows, kv_heads, 1, head_dim), (tok_rows, kv_heads, repeats, head_dim)
        )
        return spread.reshape(tok_rows, kv_heads * repeats * head_dim)

    send_key = widen(send_key)
    send_value = widen(send_value)
    key_h, value_h = (
        lax.all_to_all(send_key, "seq", split_axis=1, concat_axis=0, tiled=True),
        lax.all_to_all(send_value, "seq", split_axis=1, concat_axis=0, tiled=True),
    )
    output_h, grad_query_h, key_grad_h, value_grad_h = attend(
        query_h, key_h, value_h, grad_h, segment, 0, local_kv
    )
    attn_out, grad_queries = (
        lax.all_to_all(output_h, "seq", split_axis=0, concat_axis=1, tiled=True),
        lax.all_to_all(grad_query_h, "seq", split_axis=0, concat_axis=1, tiled=True),
    )
    key_gathered, value_gathered = (
        lax.all_to_all(key_grad_h, "seq", split_axis=0, concat_axis=1, tiled=True),
        lax.all_to_all(value_grad_h, "seq", split_axis=0, concat_axis=1, tiled=True),
    )
    key_sum = jnp.sum(key_gathered.reshape(tok_rows, kv_heads, repeats, head_dim), axis=2)
    value_sum = jnp.sum(value_gathered.reshape(tok_rows, kv_heads, repeats, head_dim), axis=2)
    key_in, value_in, scale_part = pull_tokens((key_sum, value_sum))
    grad_scale = lax.psum(scale_part, ("dp", "seq"))
    grad_keys = key_in.reshape(tok_rows, kv_heads * head_dim).astype(jnp.bfloat16)
    grad_values = value_in.reshape(tok_rows, kv_heads * head_dim).astype(jnp.bfloat16)
    return (attn_out, grad_queries, grad_keys, grad_values, grad_scale)


def solution(mesh):
    return jax.shard_map(
        on_device,
        mesh=mesh,
        in_specs=(
            P(("dp", "seq"), None),
            P(("dp", "seq"), None),
            P(("dp", "seq"), None),
            P(("dp", "seq"), None),
            P(),
            P("dp", None),
        ),
        out_specs=(
            P(("dp", "seq"), None),
            P(("dp", "seq"), None),
            P(("dp", "seq"), None),
            P(("dp", "seq"), None),
            P(),
        ),
        check_vma=False,
    )
```

profile of v0, /device:TPU:27, one launch (start us, length us, event | category | flops | bytes accessed | tf_op | source)
XLA Modules:
  0.0 368.5 jit_solution(9301017761768875349)
XLA Ops:
  4.8 6.8 %all-to-all-start.3 = ((bf16[128,8,128]{0,2,1:T(8,128)(2,1)}), bf16[128,8,128]{0,2,1:T(8,128)(2,1)S(1)}, u32[]{:S(2)}, u32[]{:S(2)}) async-start(bf16[128,8,128]{0,2,1:T(8,128)(2,1)} %bitcast.15), calls=%async_computation.3 | async-start | bytes 524288 | tf_op jit(solution)/shard_map/all_to_all | solution.py:114
  13.8 5.6 %all-to-all-done.3 = bf16[128,8,128]{0,2,1:T(8,128)(2,1)S(1)} async-done(((bf16[128,8,128]{0,2,1:T(8,128)(2,1)}), bf16[128,8,128]{0,2,1:T(8,128)(2,1)S(1)}, u32[]{:S(2)}, u32[]{:S(2)}) %all-to-all-start.3) | async-done | bytes 262176 | tf_op jit(solution)/shard_map/all_to_all | solution.py:114
  19.4 6.0 %all-to-all-start = ((bf16[128,8,512]{0,2,1:T(8,128)(2,1)}), bf16[128,8,512]{0,2,1:T(8,128)(2,1)S(1)}, u32[]{:S(2)}, u32[]{:S(2)}) async-start(bf16[128,8,512]{0,2,1:T(8,128)(2,1)} %bitcast), calls=%async_computation | async-start | bytes 2097152 | tf_op jit(solution)/shard_map/all_to_all | solution.py:100
  27.7 19.0 %all-to-all-done = bf16[128,8,512]{0,2,1:T(8,128)(2,1)S(1)} async-done(((bf16[128,8,512]{0,2,1:T(8,128)(2,1)}), bf16[128,8,512]{0,2,1:T(8,128)(2,1)S(1)}, u32[]{:S(2)}, u32[]{:S(2)}) %all-to-all-start) | async-done | bytes 1048608 | tf_op jit(solution)/shard_map/all_to_all | solution.py:100
  46.6 9.7 %all-to-all-start.2 = ((bf16[128,8,512]{0,2,1:T(8,128)(2,1)}), bf16[128,8,512]{0,2,1:T(8,128)(2,1)S(1)}, u32[]{:S(2)}, u32[]{:S(2)}) async-start(bf16[128,8,512]{0,2,1:T(8,128)(2,1)} %bitcast.263), calls=%async_computation.2 | async-start | bytes 2097152 | tf_op jit(solution)/shard_map/all_to_all | solution.py:101
  57.7 20.1 %all-to-all-done.2 = bf16[128,8,512]{0,2,1:T(8,128)(2,1)S(1)} async-done(((bf16[128,8,512]{0,2,1:T(8,128)(2,1)}), bf16[128,8,512]{0,2,1:T(8,128)(2,1)S(1)}, u32[]{:S(2)}, u32[]{:S(2)}) %all-to-all-start.2) | async-done | bytes 1048608 | tf_op jit(solution)/shard_map/all_to_all | solution.py:101
  78.5 11.1 %all-to-all-start.1 = ((bf16[128,8,128]{2,0,1:T(8,128)(2,1)}), bf16[128,8,128]{2,0,1:T(8,128)(2,1)S(1)}, u32[]{:S(2)}, u32[]{:S(2)}) async-start(bf16[128,8,128]{2,0,1:T(8,128)(2,1)} %bitcast.7), calls=%async_computation.1 | async-start | bytes 524288 | tf_op jit(solution)/shard_map/all_to_all | solution.py:113
  97.8 60.3 %while.17 = (s32[]{:T(128)}, f32[1024,1,128]{0,2,1:T(8,128)S(1)}, f32[1024,1,128]{0,2,1:T(8,128)}, bf16[2,512,1,4,128]{4,3,1,0,2:T(4,128)(2,1)}, bf16[2,512,1,4,...) while((s32[]{:T(128)}, f32[1024,1,128]{0,2,1:T(8,128)S(1)}, ...), condition=%wide.region_6.7_spmd.clone, body=%wide.region_2.6_spmd.clone.sunk | while | flops 3277318656 | bytes 84515176 | solution.py:74
  103.9 4.7 %fusion.77 = f32[1024,1,128]{0,2,1:T(8,128)} fusion(f32[1024,1,128]{0,2,1:T(8,128)} %get-tuple-element.341, bf16[1024,1,4,128]{0,3,2,1:T(8,128)(2,1)} %get-tuple-element.363, s32[]{:T(128)S(6)} %select_n.41, pred[]{:T(512)S(6)} %compare.5, f32[4,512]{1,0:T(4,128)S(1)} %fusion.74, f32[4,512]{1,0:T(4,128)S(1)} %get-tuple-element.319, ...), kind=kOutput, calls=%fused_computation.22.clone.1 | convolution fusion | flops 547618816 | bytes 10502149 | tf_op jit(solution)/shard_map/while/body/eval_jaxpr/ngqk,qngd->knd/dot_general | solution.py:68
  108.6 4.3 %multiply_reduce_fusion.4 = (f32[512,4]{0,1:T(4,128)S(1)}, bf16[4,512,128]{1,2,0:T(8,128)(2,1)S(1)}) fusion(bf16[1024,1,4,128]{0,3,2,1:T(8,128)(2,1)} %get-tuple-element.363, s32[]{:T(128)S(6)} %select_n.41, bf16[1024,1,128]{0,2,1:T(8,128)(2,1)S(1)} %get-tuple-element.364, f32[4,512]{1,0:T(4,128)S(1)} %fusion.74, ...), kind=kOutput, calls=%fused_computation.25.clone.1 | convolution fusion | flops 548665344 | bytes 10248196 | tf_op jit(solution)/shard_map/while/body/eval_jaxpr/ngqk,knd->qngd/dot_general | solution.py:54
  112.9 5.9 %fusion.75 = bf16[4,512,1024]{2,1,0:T(8,128)(2,1)} fusion(f32[4,512]{1,0:T(4,128)S(1)} %bitcast.273, f32[4,512]{1,0:T(4,128)S(1)} %fusion.74, f32[4,512]{1,0:T(4,128)S(1)} %get-tuple-element.319, f32[512,4,1024]{2,0,1:T(8,128)S(1)} %get-tuple-element.318, pred[512,1024]{1,0:T(8,128)(4,1)S(1)} %fusion.72, ...), kind=kOutput, calls=%fused_computation.10.clone.1 | convolution fusion | flops 553648128 | bytes 13918212 | tf_op jit(solution)/shard_map/while/body/eval_jaxpr/qngd,knd->ngqk/dot_general | solution.py:60
  122.3 3.4 fusion.78
  134.0 4.9 %fusion.77 = f32[1024,1,128]{0,2,1:T(8,128)} fusion(f32[1024,1,128]{0,2,1:T(8,128)} %get-tuple-element.341, bf16[1024,1,4,128]{0,3,2,1:T(8,128)(2,1)} %get-tuple-element.363, s32[]{:T(128)S(6)} %select_n.41, pred[]{:T(512)S(6)} %compare.5, f32[4,512]{1,0:T(4,128)S(1)} %fusion.74, f32[4,512]{1,0:T(4,128)S(1)} %get-tuple-element.319, ...), kind=kOutput, calls=%fused_computation.22.clone.1 | convolution fusion | flops 547618816 | bytes 10502149 | tf_op jit(solution)/shard_map/while/body/eval_jaxpr/ngqk,qngd->knd/dot_general | solution.py:68
  138.8 4.3 %multiply_reduce_fusion.4 = (f32[512,4]{0,1:T(4,128)S(1)}, bf16[4,512,128]{1,2,0:T(8,128)(2,1)S(1)}) fusion(bf16[1024,1,4,128]{0,3,2,1:T(8,128)(2,1)} %get-tuple-element.363, s32[]{:T(128)S(6)} %select_n.41, bf16[1024,1,128]{0,2,1:T(8,128)(2,1)S(1)} %get-tuple-element.364, f32[4,512]{1,0:T(4,128)S(1)} %fusion.74, ...), kind=kOutput, calls=%fused_computation.25.clone.1 | convolution fusion | flops 548665344 | bytes 10248196 | tf_op jit(solution)/shard_map/while/body/eval_jaxpr/ngqk,knd->qngd/dot_general | solution.py:54
  143.2 5.9 %fusion.75 = bf16[4,512,1024]{2,1,0:T(8,128)(2,1)} fusion(f32[4,512]{1,0:T(4,128)S(1)} %bitcast.273, f32[4,512]{1,0:T(4,128)S(1)} %fusion.74, f32[4,512]{1,0:T(4,128)S(1)} %get-tuple-element.319, f32[512,4,1024]{2,0,1:T(8,128)S(1)} %get-tuple-element.318, pred[512,1024]{1,0:T(8,128)(4,1)S(1)} %fusion.72, ...), kind=kOutput, calls=%fused_computation.10.clone.1 | convolution fusion | flops 553648128 | bytes 13918212 | tf_op jit(solution)/shard_map/while/body/eval_jaxpr/qngd,knd->ngqk/dot_general | solution.py:60
  152.6 3.4 fusion.78
  159.3 7.3 %all-to-all-start.6 = ((f32[8,128,128]{1,2,0:T(8,128)}), f32[8,128,128]{1,2,0:T(8,128)S(1)}, u32[]{:S(2)}, u32[]{:S(2)}) async-start(f32[8,128,128]{1,2,0:T(8,128)} %copy.117), calls=%async_computation.6 | async-start | bytes 1048576 | tf_op jit(solution)/shard_map/all_to_all | solution.py:124
  168.9 10.2 %all-to-all-done.6 = f32[8,128,128]{1,2,0:T(8,128)S(1)} async-done(((f32[8,128,128]{1,2,0:T(8,128)}), f32[8,128,128]{1,2,0:T(8,128)S(1)}, u32[]{:S(2)}, u32[]{:S(2)}) %all-to-all-start.6) | async-done | bytes 524320 | tf_op jit(solution)/shard_map/all_to_all | solution.py:124
  179.1 9.1 %all-to-all-start.7 = ((f32[8,128,128]{1,2,0:T(8,128)}), f32[8,128,128]{1,2,0:T(8,128)S(1)}, u32[]{:S(2)}, u32[]{:S(2)}) async-start(f32[8,128,128]{1,2,0:T(8,128)} %copy.121), calls=%async_computation.7 | async-start | bytes 1048576 | tf_op jit(solution)/shard_map/all_to_all | solution.py:125
  190.5 10.2 %all-to-all-done.7 = f32[8,128,128]{1,2,0:T(8,128)S(1)} async-done(((f32[8,128,128]{1,2,0:T(8,128)}), f32[8,128,128]{1,2,0:T(8,128)S(1)}, u32[]{:S(2)}, u32[]{:S(2)}) %all-to-all-start.7) | async-done | bytes 524320 | tf_op jit(solution)/shard_map/all_to_all | solution.py:125
  200.6 9.0 %all-to-all-start.5 = ((bf16[8,128,512]{2,1,0:T(8,128)(2,1)}), bf16[8,128,512]{2,1,0:T(8,128)(2,1)S(1)}, u32[]{:S(2)}, u32[]{:S(2)}) async-start(bf16[8,128,512]{2,1,0:T(8,128)(2,1)} %all_to_all.116), calls=%async_computation.5 | async-start | bytes 2097152 | tf_op jit(solution)/shard_map/all_to_all | solution.py:121
  210.9 22.4 %all-to-all-done.5 = bf16[8,128,512]{2,1,0:T(8,128)(2,1)S(1)} async-done(((bf16[8,128,512]{2,1,0:T(8,128)(2,1)}), bf16[8,128,512]{2,1,0:T(8,128)(2,1)S(1)}, u32[]{:S(2)}, u32[]{:S(2)}) %all-to-all-start.5) | async-done | bytes 1048608 | tf_op jit(solution)/shard_map/all_to_all | solution.py:121
  233.3 9.1 %all-to-all-start.4 = ((bf16[8,128,512]{2,1,0:T(8,128)(2,1)}), bf16[8,128,512]{2,1,0:T(8,128)(2,1)S(1)}, u32[]{:S(2)}, u32[]{:S(2)}) async-start(bf16[8,128,512]{2,1,0:T(8,128)(2,1)} %all_to_all.112), calls=%async_computation.4 | async-start | bytes 2097152 | tf_op jit(solution)/shard_map/all_to_all | solution.py:120
  247.2 117.3 %psum.7 = f32[2,4,128]{2,1,0:T(4,128)} all-reduce(f32[2,4,128]{2,1,0:T(4,128)S(1)} %pad_add_fusion), channel_id=1, replica_groups=mesh['dp'=64,'seq'=8] {'dp','seq'}, use_global_device_ids=true, to_apply=%region_13.14 | all-reduce | flops 1024 | bytes 8192 | tf_op jit(solution)/shard_map/psum | solution.py:130
  (105 shorter events, 56.3 us)
Async XLA Ops:
  0.6 55.7 %copy-start.9 = (bf16[128,512]{1,0:T(8,128)(2,1)S(1)}, bf16[128,512]{1,0:T(8,128)(2,1)}, u32[]{:S(2)}) copy-start(bf16[128,512]{1,0:T(8,128)(2,1)} %param.9) | copy-start | bytes 393220
  0.6 89.0 %copy-start.16 = (s32[1,8]{1,0:T(1,128)S(1)}, s32[1,8]{1,0:T(1,128)}, u32[]{:S(2)}) copy-start(s32[1,8]{1,0:T(1,128)} %param.13) | copy-start | bytes 100
  3.0 86.6 %copy-start = (bf16[128,512]{0,1:T(8,128)(2,1)}, bf16[128,512]{0,1:T(8,128)(2,1)S(1)}, u32[]{:S(2)}) copy-start(bf16[128,512]{0,1:T(8,128)(2,1)S(1)} %copy.107) | copy-start | bytes 393220
  4.8 14.6 %all-to-all-start.3 = ((bf16[128,8,128]{0,2,1:T(8,128)(2,1)}), bf16[128,8,128]{0,2,1:T(8,128)(2,1)S(1)}, u32[]{:S(2)}, u32[]{:S(2)}) async-start(bf16[128,8,128]{0,2,1:T(8,128)(2,1)} %bitcast.15), calls=%async_computation.3 | async-start | bytes 524288 | tf_op jit(solution)/shard_map/all_to_all | solution.py:114
  19.4 27.2 %all-to-all-start = ((bf16[128,8,512]{0,2,1:T(8,128)(2,1)}), bf16[128,8,512]{0,2,1:T(8,128)(2,1)S(1)}, u32[]{:S(2)}, u32[]{:S(2)}) async-start(bf16[128,8,512]{0,2,1:T(8,128)(2,1)} %bitcast), calls=%async_computation | async-start | bytes 2097152 | tf_op jit(solution)/shard_map/all_to_all | solution.py:100
  46.6 31.2 %all-to-all-start.2 = ((bf16[128,8,512]{0,2,1:T(8,128)(2,1)}), bf16[128,8,512]{0,2,1:T(8,128)(2,1)S(1)}, u32[]{:S(2)}, u32[]{:S(2)}) async-start(bf16[128,8,512]{0,2,1:T(8,128)(2,1)} %bitcast.263), calls=%async_computation.2 | async-start | bytes 2097152 | tf_op jit(solution)/shard_map/all_to_all | solution.py:101
  56.5 33.1 %copy-start.2 = (bf16[128,512]{0,1:T(8,128)(2,1)}, bf16[128,512]{0,1:T(8,128)(2,1)S(1)}, u32[]{:S(2)}) copy-start(bf16[128,512]{0,1:T(8,128)(2,1)S(1)} %copy.103) | copy-start | bytes 393220
  78.5 19.2 %all-to-all-start.1 = ((bf16[128,8,128]{2,0,1:T(8,128)(2,1)}), bf16[128,8,128]{2,0,1:T(8,128)(2,1)S(1)}, u32[]{:S(2)}, u32[]{:S(2)}) async-start(bf16[128,8,128]{2,0,1:T(8,128)(2,1)} %bitcast.7), calls=%async_computation.1 | async-start | bytes 524288 | tf_op jit(solution)/shard_map/all_to_all | solution.py:113
  119.2 6.6 %copy-start.4 = (bf16[2,512,1,4,128]{4,3,1,0,2:T(4,128)(2,1)S(1)}, bf16[2,512,1,4,128]{4,3,1,0,2:T(4,128)(2,1)}, u32[]{:S(2)}) copy-start(bf16[2,512,1,4,128]{4,3,1,0,2:T(4,128)(2,1)} %get-tuple-element.343) | copy-start | bytes 3145732 | tf_op jit(solution)/shard_map/while
  149.4 6.6 %copy-start.4 = (bf16[2,512,1,4,128]{4,3,1,0,2:T(4,128)(2,1)S(1)}, bf16[2,512,1,4,128]{4,3,1,0,2:T(4,128)(2,1)}, u32[]{:S(2)}) copy-start(bf16[2,512,1,4,128]{4,3,1,0,2:T(4,128)(2,1)} %get-tuple-element.343) | copy-start | bytes 3145732 | tf_op jit(solution)/shard_map/while
  149.4 6.6 %copy-start.6 = (bf16[2,512,1,4,128]{4,3,1,0,2:T(4,128)(2,1)S(1)}, bf16[2,512,1,4,128]{4,3,1,0,2:T(4,128)(2,1)}, u32[]{:S(2)}) copy-start(bf16[2,512,1,4,128]{4,3,1,0,2:T(4,128)(2,1)} %get-tuple-element.342) | copy-start | bytes 3145732 | tf_op jit(solution)/shard_map/while
  158.0 51.6 %copy-start.8 = (bf16[2,512,1,4,128]{4,3,1,0,2:T(4,128)(2,1)S(1)}, bf16[2,512,1,4,128]{4,3,1,0,2:T(4,128)(2,1)}, u32[]{:S(2)}) copy-start(bf16[2,512,1,4,128]{4,3,1,0,2:T(4,128)(2,1)} %get-tuple-element.70) | copy-start | bytes 3145732
  158.0 84.4 %copy-start.1 = (bf16[128,512]{0,1:T(8,128)(2,1)S(1)}, bf16[128,512]{0,1:T(8,128)(2,1)}, u32[]{:S(2)}) copy-start(bf16[128,512]{0,1:T(8,128)(2,1)} %copy-done) | copy-start | bytes 393220
  158.0 84.4 %copy-start.3 = (bf16[128,512]{0,1:T(8,128)(2,1)S(1)}, bf16[128,512]{0,1:T(8,128)(2,1)}, u32[]{:S(2)}) copy-start(bf16[128,512]{0,1:T(8,128)(2,1)} %copy-done.2) | copy-start | bytes 393220
  158.0 84.4 %copy-start.10 = (f32[512]{0:T(512)S(1)}, f32[512]{0:T(512)}, u32[]{:S(2)}) copy-start(f32[512]{0:T(512)} %get-tuple-element.234) | copy-start | bytes 6148
  158.0 84.4 %copy-start.11 = (f32[512]{0:T(512)S(1)}, f32[512]{0:T(512)}, u32[]{:S(2)}) copy-start(f32[512]{0:T(512)} %get-tuple-element.238) | copy-start | bytes 6148
  158.1 84.4 %copy-start.12 = (f32[512]{0:T(512)S(1)}, f32[512]{0:T(512)}, u32[]{:S(2)}) copy-start(f32[512]{0:T(512)} %get-tuple-element.232) | copy-start | bytes 6148
  158.1 84.4 %copy-start.13 = (f32[512]{0:T(512)S(1)}, f32[512]{0:T(512)}, u32[]{:S(2)}) copy-start(f32[512]{0:T(512)} %get-tuple-element.235) | copy-start | bytes 6148
  158.1 84.4 %copy-start.14 = (f32[512]{0:T(512)S(1)}, f32[512]{0:T(512)}, u32[]{:S(2)}) copy-start(f32[512]{0:T(512)} %get-tuple-element.236) | copy-start | bytes 6148
  158.1 84.4 %copy-start.15 = (f32[512]{0:T(512)S(1)}, f32[512]{0:T(512)}, u32[]{:S(2)}) copy-start(f32[512]{0:T(512)} %get-tuple-element.239) | copy-start | bytes 6148
  159.3 19.8 %all-to-all-start.6 = ((f32[8,128,128]{1,2,0:T(8,128)}), f32[8,128,128]{1,2,0:T(8,128)S(1)}, u32[]{:S(2)}, u32[]{:S(2)}) async-start(f32[8,128,128]{1,2,0:T(8,128)} %copy.117), calls=%async_computation.6 | async-start | bytes 1048576 | tf_op jit(solution)/shard_map/all_to_all | solution.py:124
  179.1 21.5 %all-to-all-start.7 = ((f32[8,128,128]{1,2,0:T(8,128)}), f32[8,128,128]{1,2,0:T(8,128)S(1)}, u32[]{:S(2)}, u32[]{:S(2)}) async-start(f32[8,128,128]{1,2,0:T(8,128)} %copy.121), calls=%async_computation.7 | async-start | bytes 1048576 | tf_op jit(solution)/shard_map/all_to_all | solution.py:125
  200.6 32.7 %all-to-all-start.5 = ((bf16[8,128,512]{2,1,0:T(8,128)(2,1)}), bf16[8,128,512]{2,1,0:T(8,128)(2,1)S(1)}, u32[]{:S(2)}, u32[]{:S(2)}) async-start(bf16[8,128,512]{2,1,0:T(8,128)(2,1)} %all_to_all.116), calls=%async_computation.5 | async-start | bytes 2097152 | tf_op jit(solution)/shard_map/all_to_all | solution.py:121
  233.3 133.2 %all-to-all-start.4 = ((bf16[8,128,512]{2,1,0:T(8,128)(2,1)}), bf16[8,128,512]{2,1,0:T(8,128)(2,1)S(1)}, u32[]{:S(2)}, u32[]{:S(2)}) async-start(bf16[8,128,512]{2,1,0:T(8,128)(2,1)} %all_to_all.112), calls=%async_computation.4 | async-start | bytes 2097152 | tf_op jit(solution)/shard_map/all_to_all | solution.py:120
  (5 other events, 11.2 us)
where the time goes:
time: 370 us; the launch traced here: 368 us
  blocking collectives  117 us (32%)
  waiting for transfers between devices  87.9 us (24%)
  starting transfers between devices  68.1 us (18%)
  matrix products  46.9 us (13%)
  local copies, waits for them, and re-layouts  33.1 us (9%)
  other arithmetic  12.8 us (3%)
    psum x1, blocking collectives, on_device(): grad_scale = lax.psum(scale_part, ('dp', 'seq'))  117 us
    all_to_all x1, waiting for transfers between devices, on_device(): lax.all_to_all(grad_query_h, 'seq', split_axis=0, concat_axis=1, tiled=True)  22.4 us
    all_to_all x1, waiting for transfers between devices, on_device(): lax.all_to_all(grad_out, 'seq', split_axis=1, concat_axis=0, tiled=True)  20.1 us
    all_to_all x1, waiting for transfers between devices, on_device(): lax.all_to_all(queries, 'seq', split_axis=1, concat_axis=0, tiled=True)  19 us
    dot_general x2, matrix products, step(): jnp.einsum('qngd,knd->ngqk', grad_blk, value3, preferred_element_type=jnp...  11.8 us
    all_to_all x1, starting transfers between devices, on_device(): lax.all_to_all(send_key, 'seq', split_axis=1, concat_axis=0, tiled=True)  11.1 us
    all_to_all x1, waiting for transfers between devices, on_device(): lax.all_to_all(key_grad_h, 'seq', split_axis=0, concat_axis=1, tiled=True)  10.2 us
    all_to_all x1, waiting for transfers between devices, on_device(): lax.all_to_all(value_grad_h, 'seq', split_axis=0, concat_axis=1, tiled=True)  10.2 us
  transfers between devices with their start and end apart: 8, of which 7 were waited for; matrix products, arithmetic and copies ran while one was open for 6% of the time, Pallas kernels for 0%

commit v1 on v0

--- a/solution.py
+++ b/solution.py
@@ -127,7 +127,7 @@
     key_sum = jnp.sum(key_gathered.reshape(tok_rows, kv_heads, repeats, head_dim), axis=2)
     value_sum = jnp.sum(value_gathered.reshape(tok_rows, kv_heads, repeats, head_dim), axis=2)
     key_in, value_in, scale_part = pull_tokens((key_sum, value_sum))
-    grad_scale = lax.psum(scale_part, ("dp", "seq"))
+    grad_scale = jnp.sum(lax.all_gather(scale_part, ("dp", "seq")), axis=0)
     grad_keys = key_in.reshape(tok_rows, kv_heads * head_dim).astype(jnp.bfloat16)
     grad_values = value_in.reshape(tok_rows, kv_heads * head_dim).astype(jnp.bfloat16)
     return (attn_out, grad_queries, grad_keys, grad_values, grad_scale)

time: 370 us -> 353 us (0.954)
  the two profiles are of different devices: /device:TPU:27 before, /device:TPU:1 now
where the time goes in v1:
time: 353 us; the launch traced here: 352 us
  waiting for transfers between devices  204 us (58%)
  matrix products  46.9 us (13%)
  starting transfers between devices  34.7 us (10%)
  local copies, waits for them, and re-layouts  33.7 us (10%)
  other arithmetic  16.1 us (5%)
  between operations  14.4 us (4%)
    all_gather x1, waiting for transfers between devices, on_device(): grad_scale = jnp.sum(lax.all_gather(scale_part, ('dp', 'seq')), axis=0)  81.8 us
    all_to_all x1, waiting for transfers between devices, on_device(): lax.all_to_all(grad_out, 'seq', split_axis=1, concat_axis=0, tiled=True)  24.7 us
    all_to_all x1, waiting for transfers between devices, on_device(): lax.all_to_all(queries, 'seq', split_axis=1, concat_axis=0, tiled=True)  23.7 us
    all_to_all x1, waiting for transfers between devices, on_device(): lax.all_to_all(grad_query_h, 'seq', split_axis=0, concat_axis=1, tiled=True)  22 us
    all_to_all x1, waiting for transfers between devices, on_device(): lax.all_to_all(output_h, 'seq', split_axis=0, concat_axis=1, tiled=True)  21.3 us
    all_to_all x1, waiting for transfers between devices, on_device(): lax.all_to_all(value_grad_h, 'seq', split_axis=0, concat_axis=1, tiled=True)  12.2 us
    dot_general x2, matrix products, step(): jnp.einsum('qngd,knd->ngqk', grad_blk, value3, preferred_element_type=jnp...  11.8 us
    unnamed x37, local copies, waits for them, and re-layouts  10.7 us
  transfers between devices with their start and end apart: 9, of which 9 were waited for; matrix products, arithmetic and copies ran while one was open for 6% of the time, Pallas kernels for 0%

profile of v1, /device:TPU:1, one launch (start us, length us, event | category | flops | bytes accessed | tf_op | source)
XLA Modules:
  0.0 351.7 jit_solution(1963060574241853637)
XLA Ops:
  11.3 7.7 %all-to-all-start.3 = ((bf16[128,8,128]{0,2,1:T(8,128)(2,1)}), bf16[128,8,128]{0,2,1:T(8,128)(2,1)S(1)}, u32[]{:S(2)}, u32[]{:S(2)}) async-start(bf16[128,8,128]{0,2,1:T(8,128)(2,1)} %bitcast.15), calls=%async_computation.3 | async-start | bytes 524288 | tf_op jit(solution)/shard_map/all_to_all | solution.py:114
  21.3 7.1 %all-to-all-done.3 = bf16[128,8,128]{0,2,1:T(8,128)(2,1)S(1)} async-done(((bf16[128,8,128]{0,2,1:T(8,128)(2,1)}), bf16[128,8,128]{0,2,1:T(8,128)(2,1)S(1)}, u32[]{:S(2)}, u32[]{:S(2)}) %all-to-all-start.3) | async-done | bytes 262176 | tf_op jit(solution)/shard_map/all_to_all | solution.py:114
  28.4 3.6 %all-to-all-start = ((bf16[128,8,512]{0,2,1:T(8,128)(2,1)}), bf16[128,8,512]{0,2,1:T(8,128)(2,1)S(1)}, u32[]{:S(2)}, u32[]{:S(2)}) async-start(bf16[128,8,512]{0,2,1:T(8,128)(2,1)} %bitcast), calls=%async_computation | async-start | bytes 2097152 | tf_op jit(solution)/shard_map/all_to_all | solution.py:100
  34.2 23.7 %all-to-all-done = bf16[128,8,512]{0,2,1:T(8,128)(2,1)S(1)} async-done(((bf16[128,8,512]{0,2,1:T(8,128)(2,1)}), bf16[128,8,512]{0,2,1:T(8,128)(2,1)S(1)}, u32[]{:S(2)}, u32[]{:S(2)}) %all-to-all-start) | async-done | bytes 1048608 | tf_op jit(solution)/shard_map/all_to_all | solution.py:100
  58.0 3.6 %all-to-all-start.2 = ((bf16[128,8,512]{0,2,1:T(8,128)(2,1)}), bf16[128,8,512]{0,2,1:T(8,128)(2,1)S(1)}, u32[]{:S(2)}, u32[]{:S(2)}) async-start(bf16[128,8,512]{0,2,1:T(8,128)(2,1)} %bitcast.264), calls=%async_computation.2 | async-start | bytes 2097152 | tf_op jit(solution)/shard_map/all_to_all | solution.py:101
  62.8 24.7 %all-to-all-done.2 = bf16[128,8,512]{0,2,1:T(8,128)(2,1)S(1)} async-done(((bf16[128,8,512]{0,2,1:T(8,128)(2,1)}), bf16[128,8,512]{0,2,1:T(8,128)(2,1)S(1)}, u32[]{:S(2)}, u32[]{:S(2)}) %all-to-all-start.2) | async-done | bytes 1048608 | tf_op jit(solution)/shard_map/all_to_all | solution.py:101
  101.2 60.3 %while.17 = (s32[]{:T(128)}, f32[1024,1,128]{0,2,1:T(8,128)S(1)}, f32[1024,1,128]{0,2,1:T(8,128)}, bf16[2,512,1,4,128]{4,3,1,0,2:T(4,128)(2,1)}, bf16[2,512,1,4,...) while((s32[]{:T(128)}, f32[1024,1,128]{0,2,1:T(8,128)S(1)}, ...), condition=%wide.region_6.7_spmd.clone, body=%wide.region_2.6_spmd.clone.sunk | while | flops 3277318656 | bytes 84515176 | solution.py:74
  107.4 4.7 %fusion.77 = f32[1024,1,128]{0,2,1:T(8,128)} fusion(f32[1024,1,128]{0,2,1:T(8,128)} %get-tuple-element.341, bf16[1024,1,4,128]{0,3,2,1:T(8,128)(2,1)} %get-tuple-element.363, s32[]{:T(128)S(6)} %select_n.41, pred[]{:T(512)S(6)} %compare.5, f32[4,512]{1,0:T(4,128)S(1)} %fusion.74, f32[4,512]{1,0:T(4,128)S(1)} %get-tuple-element.319, ...), kind=kOutput, calls=%fused_computation.22.clone.1 | convolution fusion | flops 547618816 | bytes 10502149 | tf_op jit(solution)/shard_map/while/body/eval_jaxpr/ngqk,qngd->knd/dot_general | solution.py:68
  112.1 4.3 %multiply_reduce_fusion.4 = (f32[512,4]{0,1:T(4,128)S(1)}, bf16[4,512,128]{1,2,0:T(8,128)(2,1)S(1)}) fusion(bf16[1024,1,4,128]{0,3,2,1:T(8,128)(2,1)} %get-tuple-element.363, s32[]{:T(128)S(6)} %select_n.41, bf16[1024,1,128]{0,2,1:T(8,128)(2,1)S(1)} %get-tuple-element.364, f32[4,512]{1,0:T(4,128)S(1)} %fusion.74, ...), kind=kOutput, calls=%fused_computation.25.clone.1 | convolution fusion | flops 548665344 | bytes 10248196 | tf_op jit(solution)/shard_map/while/body/eval_jaxpr/ngqk,knd->qngd/dot_general | solution.py:54
  116.5 5.9 %fusion.75 = bf16[4,512,1024]{2,1,0:T(8,128)(2,1)} fusion(f32[4,512]{1,0:T(4,128)S(1)} %bitcast.275, f32[4,512]{1,0:T(4,128)S(1)} %fusion.74, f32[4,512]{1,0:T(4,128)S(1)} %get-tuple-element.319, f32[512,4,1024]{2,0,1:T(8,128)S(1)} %get-tuple-element.318, pred[512,1024]{1,0:T(8,128)(4,1)S(1)} %fusion.72, ...), kind=kOutput, calls=%fused_computation.10.clone.1 | convolution fusion | flops 553648128 | bytes 13918212 | tf_op jit(solution)/shard_map/while/body/eval_jaxpr/qngd,knd->ngqk/dot_general | solution.py:60
  125.8 3.4 fusion.78
  137.4 4.8 %fusion.77 = f32[1024,1,128]{0,2,1:T(8,128)} fusion(f32[1024,1,128]{0,2,1:T(8,128)} %get-tuple-element.341, bf16[1024,1,4,128]{0,3,2,1:T(8,128)(2,1)} %get-tuple-element.363, s32[]{:T(128)S(6)} %select_n.41, pred[]{:T(512)S(6)} %compare.5, f32[4,512]{1,0:T(4,128)S(1)} %fusion.74, f32[4,512]{1,0:T(4,128)S(1)} %get-tuple-element.319, ...), kind=kOutput, calls=%fused_computation.22.clone.1 | convolution fusion | flops 547618816 | bytes 10502149 | tf_op jit(solution)/shard_map/while/body/eval_jaxpr/ngqk,qngd->knd/dot_general | solution.py:68
  142.2 4.3 %multiply_reduce_fusion.4 = (f32[512,4]{0,1:T(4,128)S(1)}, bf16[4,512,128]{1,2,0:T(8,128)(2,1)S(1)}) fusion(bf16[1024,1,4,128]{0,3,2,1:T(8,128)(2,1)} %get-tuple-element.363, s32[]{:T(128)S(6)} %select_n.41, bf16[1024,1,128]{0,2,1:T(8,128)(2,1)S(1)} %get-tuple-element.364, f32[4,512]{1,0:T(4,128)S(1)} %fusion.74, ...), kind=kOutput, calls=%fused_computation.25.clone.1 | convolution fusion | flops 548665344 | bytes 10248196 | tf_op jit(solution)/shard_map/while/body/eval_jaxpr/ngqk,knd->qngd/dot_general | solution.py:54
  146.6 5.9 %fusion.75 = bf16[4,512,1024]{2,1,0:T(8,128)(2,1)} fusion(f32[4,512]{1,0:T(4,128)S(1)} %bitcast.275, f32[4,512]{1,0:T(4,128)S(1)} %fusion.74, f32[4,512]{1,0:T(4,128)S(1)} %get-tuple-element.319, f32[512,4,1024]{2,0,1:T(8,128)S(1)} %get-tuple-element.318, pred[512,1024]{1,0:T(8,128)(4,1)S(1)} %fusion.72, ...), kind=kOutput, calls=%fused_computation.10.clone.1 | convolution fusion | flops 553648128 | bytes 13918212 | tf_op jit(solution)/shard_map/while/body/eval_jaxpr/qngd,knd->ngqk/dot_general | solution.py:60
  156.0 3.4 fusion.78
  162.6 5.6 %all-to-all-start.6 = ((f32[8,128,128]{1,2,0:T(8,128)}), f32[8,128,128]{1,2,0:T(8,128)S(1)}, u32[]{:S(2)}, u32[]{:S(2)}) async-start(f32[8,128,128]{1,2,0:T(8,128)} %copy.117), calls=%async_computation.6 | async-start | bytes 1048576 | tf_op jit(solution)/shard_map/all_to_all | solution.py:124
  170.5 10.5 %all-to-all-done.6 = f32[8,128,128]{1,2,0:T(8,128)S(1)} async-done(((f32[8,128,128]{1,2,0:T(8,128)}), f32[8,128,128]{1,2,0:T(8,128)S(1)}, u32[]{:S(2)}, u32[]{:S(2)}) %all-to-all-start.6) | async-done | bytes 524320 | tf_op jit(solution)/shard_map/all_to_all | solution.py:124
  181.0 3.7 %all-to-all-start.7 = ((f32[8,128,128]{1,2,0:T(8,128)}), f32[8,128,128]{1,2,0:T(8,128)S(1)}, u32[]{:S(2)}, u32[]{:S(2)}) async-start(f32[8,128,128]{1,2,0:T(8,128)} %copy.121), calls=%async_computation.7 | async-start | bytes 1048576 | tf_op jit(solution)/shard_map/all_to_all | solution.py:125
  184.8 12.2 %all-to-all-done.7 = f32[8,128,128]{1,2,0:T(8,128)S(1)} async-done(((f32[8,128,128]{1,2,0:T(8,128)}), f32[8,128,128]{1,2,0:T(8,128)S(1)}, u32[]{:S(2)}, u32[]{:S(2)}) %all-to-all-start.7) | async-done | bytes 524320 | tf_op jit(solution)/shard_map/all_to_all | solution.py:125
  201.8 3.6 %all-to-all-start.5 = ((bf16[8,128,512]{2,1,0:T(8,128)(2,1)}), bf16[8,128,512]{2,1,0:T(8,128)(2,1)S(1)}, u32[]{:S(2)}, u32[]{:S(2)}) async-start(bf16[8,128,512]{2,1,0:T(8,128)(2,1)} %all_to_all.116), calls=%async_computation.5 | async-start | bytes 2097152 | tf_op jit(solution)/shard_map/all_to_all | solution.py:121
  207.7 22.0 %all-to-all-done.5 = bf16[8,128,512]{2,1,0:T(8,128)(2,1)S(1)} async-done(((bf16[8,128,512]{2,1,0:T(8,128)(2,1)}), bf16[8,128,512]{2,1,0:T(8,128)(2,1)S(1)}, u32[]{:S(2)}, u32[]{:S(2)}) %all-to-all-start.5) | async-done | bytes 1048608 | tf_op jit(solution)/shard_map/all_to_all | solution.py:121
  229.7 3.6 %all-to-all-start.4 = ((bf16[8,128,512]{2,1,0:T(8,128)(2,1)}), bf16[8,128,512]{2,1,0:T(8,128)(2,1)S(1)}, u32[]{:S(2)}, u32[]{:S(2)}) async-start(bf16[8,128,512]{2,1,0:T(8,128)(2,1)} %all_to_all.112), calls=%async_computation.4 | async-start | bytes 2097152 | tf_op jit(solution)/shard_map/all_to_all | solution.py:120
  237.1 21.3 %all-to-all-done.4 = bf16[8,128,512]{2,1,0:T(8,128)(2,1)S(1)} async-done(((bf16[8,128,512]{2,1,0:T(8,128)(2,1)}), bf16[8,128,512]{2,1,0:T(8,128)(2,1)S(1)}, u32[]{:S(2)}, u32[]{:S(2)}) %all-to-all-start.4) | async-done | bytes 1048608 | tf_op jit(solution)/shard_map/all_to_all | solution.py:120
  260.3 81.8 %all-gather.3.cloned.1.call-done = f32[1024,4,128]{2,1,0:T(4,128)} async-done(((f32[2,4,128]{2,1,0:T(4,128)}), f32[1024,4,128]{2,1,0:T(4,128)}) %all-gather.3.cloned.1.call-update) | async-done | bytes 2097168 | tf_op jit(solution)/shard_map/all_gather | solution.py:130
  (110 shorter events, 64.3 us)
Async XLA Ops:
  7.2 54.4 %copy-start.10 = (bf16[128,512]{1,0:T(8,128)(2,1)S(1)}, bf16[128,512]{1,0:T(8,128)(2,1)}, u32[]{:S(2)}) copy-start(bf16[128,512]{1,0:T(8,128)(2,1)} %param.9) | copy-start | bytes 393220
  7.2 84.6 %copy-start.17 = (s32[1,8]{1,0:T(1,128)S(1)}, s32[1,8]{1,0:T(1,128)}, u32[]{:S(2)}) copy-start(s32[1,8]{1,0:T(1,128)} %param.13) | copy-start | bytes 100
  9.6 82.1 %copy-start = (bf16[128,512]{0,1:T(8,128)(2,1)}, bf16[128,512]{0,1:T(8,128)(2,1)S(1)}, u32[]{:S(2)}) copy-start(bf16[128,512]{0,1:T(8,128)(2,1)S(1)} %copy.107) | copy-start | bytes 393220
  11.3 17.1 %all-to-all-start.3 = ((bf16[128,8,128]{0,2,1:T(8,128)(2,1)}), bf16[128,8,128]{0,2,1:T(8,128)(2,1)S(1)}, u32[]{:S(2)}, u32[]{:S(2)}) async-start(bf16[128,8,128]{0,2,1:T(8,128)(2,1)} %bitcast.15), calls=%async_computation.3 | async-start | bytes 524288 | tf_op jit(solution)/shard_map/all_to_all | solution.py:114
  28.4 29.6 %all-to-all-start = ((bf16[128,8,512]{0,2,1:T(8,128)(2,1)}), bf16[128,8,512]{0,2,1:T(8,128)(2,1)S(1)}, u32[]{:S(2)}, u32[]{:S(2)}) async-start(bf16[128,8,512]{0,2,1:T(8,128)(2,1)} %bitcast), calls=%async_computation | async-start | bytes 2097152 | tf_op jit(solution)/shard_map/all_to_all | solution.py:100
  58.0 29.6 %all-to-all-start.2 = ((bf16[128,8,512]{0,2,1:T(8,128)(2,1)}), bf16[128,8,512]{0,2,1:T(8,128)(2,1)S(1)}, u32[]{:S(2)}, u32[]{:S(2)}) async-start(bf16[128,8,512]{0,2,1:T(8,128)(2,1)} %bitcast.264), calls=%async_computation.2 | async-start | bytes 2097152 | tf_op jit(solution)/shard_map/all_to_all | solution.py:101
  61.7 30.0 %copy-start.2 = (bf16[128,512]{0,1:T(8,128)(2,1)}, bf16[128,512]{0,1:T(8,128)(2,1)S(1)}, u32[]{:S(2)}) copy-start(bf16[128,512]{0,1:T(8,128)(2,1)S(1)} %copy.103) | copy-start | bytes 393220
  88.3 12.8 %all-to-all-start.1 = ((bf16[128,8,128]{2,0,1:T(8,128)(2,1)}), bf16[128,8,128]{2,0,1:T(8,128)(2,1)S(1)}, u32[]{:S(2)}, u32[]{:S(2)}) async-start(bf16[128,8,128]{2,0,1:T(8,128)(2,1)} %bitcast.7), calls=%async_computation.1 | async-start | bytes 524288 | tf_op jit(solution)/shard_map/all_to_all | solution.py:113
  93.1 8.0 %copy-start.9 = (bf16[1024,1,128]{0,2,1:T(8,128)(2,1)S(1)}, bf16[1024,1,128]{0,2,1:T(8,128)(2,1)}, u32[]{:S(2)}) copy-start(bf16[1024,1,128]{0,2,1:T(8,128)(2,1)} %copy.111) | copy-start | bytes 786436
  101.1 95.9 %copy-start.1 = (bf16[128,512]{0,1:T(8,128)(2,1)S(1)}, bf16[128,512]{0,1:T(8,128)(2,1)}, u32[]{:S(2)}) copy-start(bf16[128,512]{0,1:T(8,128)(2,1)} %copy-done) | copy-start | bytes 393220
  101.1 95.9 %copy-start.3 = (bf16[128,512]{0,1:T(8,128)(2,1)S(1)}, bf16[128,512]{0,1:T(8,128)(2,1)}, u32[]{:S(2)}) copy-start(bf16[128,512]{0,1:T(8,128)(2,1)} %copy-done.2) | copy-start | bytes 393220
  101.1 95.9 %copy-start.11 = (f32[512]{0:T(512)S(1)}, f32[512]{0:T(512)}, u32[]{:S(2)}) copy-start(f32[512]{0:T(512)} %get-tuple-element.234) | copy-start | bytes 6148
  101.1 95.9 %copy-start.12 = (f32[512]{0:T(512)S(1)}, f32[512]{0:T(512)}, u32[]{:S(2)}) copy-start(f32[512]{0:T(512)} %get-tuple-element.238) | copy-start | bytes 6148
  101.1 95.9 %copy-start.13 = (f32[512]{0:T(512)S(1)}, f32[512]{0:T(512)}, u32[]{:S(2)}) copy-start(f32[512]{0:T(512)} %get-tuple-element.232) | copy-start | bytes 6148
  101.1 95.9 %copy-start.14 = (f32[512]{0:T(512)S(1)}, f32[512]{0:T(512)}, u32[]{:S(2)}) copy-start(f32[512]{0:T(512)} %get-tuple-element.235) | copy-start | bytes 6148
  101.1 95.9 %copy-start.15 = (f32[512]{0:T(512)S(1)}, f32[512]{0:T(512)}, u32[]{:S(2)}) copy-start(f32[512]{0:T(512)} %get-tuple-element.236) | copy-start | bytes 6148
  101.2 95.9 %copy-start.16 = (f32[512]{0:T(512)S(1)}, f32[512]{0:T(512)}, u32[]{:S(2)}) copy-start(f32[512]{0:T(512)} %get-tuple-element.239) | copy-start | bytes 6148
  122.7 6.6 %copy-start.4 = (bf16[2,512,1,4,128]{4,3,1,0,2:T(4,128)(2,1)S(1)}, bf16[2,512,1,4,128]{4,3,1,0,2:T(4,128)(2,1)}, u32[]{:S(2)}) copy-start(bf16[2,512,1,4,128]{4,3,1,0,2:T(4,128)(2,1)} %get-tuple-element.343) | copy-start | bytes 3145732 | tf_op jit(solution)/shard_map/while
  161.4 39.2 %copy-start.6 = (bf16[2,512,1,4,128]{4,3,1,0,2:T(4,128)(2,1)S(1)}, bf16[2,512,1,4,128]{4,3,1,0,2:T(4,128)(2,1)}, u32[]{:S(2)}) copy-start(bf16[2,512,1,4,128]{4,3,1,0,2:T(4,128)(2,1)} %get-tuple-element.71) | copy-start | bytes 3145732
  162.6 18.4 %all-to-all-start.6 = ((f32[8,128,128]{1,2,0:T(8,128)}), f32[8,128,128]{1,2,0:T(8,128)S(1)}, u32[]{:S(2)}, u32[]{:S(2)}) async-start(f32[8,128,128]{1,2,0:T(8,128)} %copy.117), calls=%async_computation.6 | async-start | bytes 1048576 | tf_op jit(solution)/shard_map/all_to_all | solution.py:124
  181.0 16.0 %all-to-all-start.7 = ((f32[8,128,128]{1,2,0:T(8,128)}), f32[8,128,128]{1,2,0:T(8,128)S(1)}, u32[]{:S(2)}, u32[]{:S(2)}) async-start(f32[8,128,128]{1,2,0:T(8,128)} %copy.121), calls=%async_computation.7 | async-start | bytes 1048576 | tf_op jit(solution)/shard_map/all_to_all | solution.py:125
  184.7 157.4 %all-gather.3.cloned.1.call-start = ((), (), s32[]{:S(2)}) async-start(), calls=%async_computation.8 | async-start | bytes 2101248 | tf_op jit(solution)/shard_map/all_gather | solution.py:130
  201.8 27.8 %all-to-all-start.5 = ((bf16[8,128,512]{2,1,0:T(8,128)(2,1)}), bf16[8,128,512]{2,1,0:T(8,128)(2,1)S(1)}, u32[]{:S(2)}, u32[]{:S(2)}) async-start(bf16[8,128,512]{2,1,0:T(8,128)(2,1)} %all_to_all.116), calls=%async_computation.5 | async-start | bytes 2097152 | tf_op jit(solution)/shard_map/all_to_all | solution.py:121
  229.7 28.7 %all-to-all-start.4 = ((bf16[8,128,512]{2,1,0:T(8,128)(2,1)}), bf16[8,128,512]{2,1,0:T(8,128)(2,1)S(1)}, u32[]{:S(2)}, u32[]{:S(2)}) async-start(bf16[8,128,512]{2,1,0:T(8,128)(2,1)} %all_to_all.112), calls=%async_computation.4 | async-start | bytes 2097152 | tf_op jit(solution)/shard_map/all_to_all | solution.py:120
  (7 other events, 24.5 us)
Sparse Core Ops, SparseCore 0:
  200.7 141.3 all-gather.2
